TPU v7x, 128 devices: a whole 4x4x4 slice. The times are simulated.
128 devices in a mesh: seq: 8 (over z, y_hi), grp: 16 (over y_lo, x, core).
Axes of the slice: x: 4, y: 4 (y_hi: 2, y_lo: 2; y = y_hi * 2 + y_lo), z: 4, core: 2. Of those that a mesh axis runs over, the one named last changes fastest.
Arguments:
- self_query: bfloat16 [16, 1024, 5120], P('grp', 'seq'), may hold values from -250 to 250
- self_key: bfloat16 [16, 1024, 5120], P('grp', 'seq'), may hold values from -12 to 12
- self_value: bfloat16 [16, 1024, 5120], P('grp', 'seq'), may hold values from -6 to 6
- self_upstream: bfloat16 [16, 1024, 5120], P('grp', 'seq'), may hold values from -6 to 6
- cross_query: bfloat16 [16, 1024, 5120], P('grp', 'seq'), may hold values from -250 to 250
- context_key: bfloat16 [512, 5120], replicated, may hold values from -12 to 12
- context_value: bfloat16 [512, 5120], replicated, may hold values from -6 to 6
- cross_upstream: bfloat16 [16, 1024, 5120], P('grp', 'seq'), may hold values from -6 to 6
Outputs:
- query_grad: bfloat16 [16, 1024, 5120], P('grp', 'seq')
- key_grad: bfloat16 [16, 1024, 5120], P('grp', 'seq')
- value_grad: bfloat16 [16, 1024, 5120], P('grp', 'seq')
- cross_query_grad: bfloat16 [16, 1024, 5120], P('grp', 'seq')
- context_key_grad: float32 [512, 5120], P(None, 'seq')
- context_value_grad: float32 [512, 5120], P(None, 'seq')
All inputs are finite; a program needn't handle non-finite values.
Results may differ from a plain program's by a relative error of at most 0.013.
Values may be sent and summed in bfloat16 or wider, within the bound.
A program may use at most 256 MiB of HBM per device.

v0:
```python
import jax
import jax.numpy as jnp
from jax import lax
from jax.sharding import PartitionSpec as P

HD = 128


def pick_rows(row_count, largest):
    block_rows = min(largest, row_count)
    while row_count % block_rows:
        block_rows = block_rows - 1
    return block_rows


def block_backward(queries, key_in, value_in, upstream):
    row_count, head_count, head_depth = queries.shape
    block_rows = pick_rows(row_count, 512)
    block_count = row_count // block_rows
    piece_rows = pick_rows(block_rows, 128)
    piece_count = block_rows // piece_rows
    scaling = HD ** (-0.5)

    def advance(totals, pieces):
        query_block, upstream_block = pieces
        scores = (
            jnp.einsum("nhe,mhe->hnm", query_block, key_in, preferred_element_type=jnp.float32)
            * scaling
        )
        weights = jax.nn.softmax(scores, axis=-1)
        rounded = weights.astype(jnp.bfloat16)
        output = jnp.einsum("hnm,mhe->nhe", rounded, value_in, preferred_element_type=jnp.float32)
        row_inner = jnp.sum(upstream_block.astype(jnp.float32) * output, axis=-1)
        grad_prob = jnp.einsum(
            "nhe,mhe->hnm", upstream_block, value_in, preferred_element_type=jnp.float32
        )
        grad_score = (
            weights * (grad_prob - jnp.transpose(row_inner)[:, :, None]) * scaling
        ).astype(jnp.bfloat16)
        query_grad = jnp.einsum(
            "hnm,mhe->nhe", grad_score, key_in, preferred_element_type=jnp.float32
        ).astype(jnp.bfloat16)
        score_split = grad_score.reshape(head_count, piece_count, piece_rows, grad_score.shape[2])
        weight_split = rounded.reshape(head_count, piece_count, piece_rows, rounded.shape[2])
        query_split = query_block.reshape(piece_count, piece_rows, head_count, head_depth)
        upstream_split = upstream_block.reshape(piece_count, piece_rows, head_count, head_depth)
        key_terms = jnp.einsum(
            "hgnm,gnhe->gmhe", score_split, query_split, preferred_element_type=jnp.float32
        )
        value_terms = jnp.einsum(
            "hgnm,gnhe->gmhe", weight_split, upstream_split, preferred_element_type=jnp.float32
        )
        key_sum = totals[0] + jnp.sum(key_terms, axis=0)
        value_sum = totals[1] + jnp.sum(value_terms, axis=0)
        return ((key_sum, value_sum), query_grad)

    zero_sum = jnp.zeros(key_in.shape, jnp.float32)
    blocked = (
        queries.reshape(block_count, block_rows, head_count, head_depth),
        upstream.reshape(block_count, block_rows, head_count, head_depth),
    )
    running, query_grads = lax.scan(advance, (zero_sum, zero_sum), blocked)
    return (query_grads.reshape(row_count, head_count, head_depth), running[0], running[1])


def shards(
    self_query,
    self_key,
    self_value,
    self_upstream,
    cross_query,
    context_key,
    context_value,
    cross_upstream,
):
    token_count = self_query.shape[1]
    full_width = self_query.shape[2]
    head_count = full_width // HD
    text_rows = context_key.shape[0]
    seq_count = lax.axis_size("seq")
    group_heads = head_count // seq_count

    def to_heads(tensor):
        return tensor.reshape(token_count, head_count, HD)

    def to_groups(tensor):
        return tensor.reshape(token_count, seq_count, group_heads, HD)

    pieces = (
        lax.all_to_all(to_groups(self_query[0]), "seq", split_axis=1, concat_axis=0, tiled=True),
        lax.all_to_all(to_groups(self_key[0]), "seq", split_axis=1, concat_axis=0, tiled=True),
        lax.all_to_all(to_groups(self_value[0]), "seq", split_axis=1, concat_axis=0, tiled=True),
        lax.all_to_all(to_groups(self_upstream[0]), "seq", split_axis=1, concat_axis=0, tiled=True),
    )
    rows = pieces[0].shape[0]
    items = pieces[0].shape[2]

    def flat(tensor):
        return tensor.reshape(rows, items, HD)

    query_part, key_part, value_part = block_backward(
        flat(pieces[0]), flat(pieces[1]), flat(pieces[2]), flat(pieces[3])
    )
    shape_back = (rows, 1, items, HD)
    query_grad, key_grad, value_grad = (
        lax.all_to_all(
            query_part.reshape(shape_back), "seq", split_axis=0, concat_axis=1, tiled=True
        ),
        lax.all_to_all(
            key_part.astype(jnp.bfloat16).reshape(shape_back),
            "seq",
            split_axis=0,
            concat_axis=1,
            tiled=True,
        ),
        lax.all_to_all(
            value_part.astype(jnp.bfloat16).reshape(shape_back),
            "seq",
            split_axis=0,
            concat_axis=1,
            tiled=True,
        ),
    )
    columns = full_width // seq_count
    offset = lax.axis_index("seq") * columns
    context_heads = context_key.reshape(text_rows, head_count, HD)
    value_heads = context_value.reshape(text_rows, head_count, HD)
    cross_grad, context_keys_part, context_values_part = block_backward(
        to_heads(cross_query[0]), context_heads, value_heads, to_heads(cross_upstream[0])
    )
    key_partial = context_keys_part.reshape(text_rows, full_width)
    value_partial = context_values_part.reshape(text_rows, full_width)
    key_whole, value_whole = lax.psum((key_partial, value_partial), ("seq", "grp"))
    key_total = lax.dynamic_slice_in_dim(key_whole, offset, columns, 1)
    value_total = lax.dynamic_slice_in_dim(value_whole, offset, columns, 1)
    shape_out = (1, token_count, full_width)
    return (
        query_grad.reshape(shape_out),
        key_grad.reshape(shape_out),
        value_grad.reshape(shape_out),
        cross_grad.reshape(shape_out),
        key_total,
        value_total,
    )


def solution(mesh):
    return jax.shard_map(
        shards,
        mesh=mesh,
        in_specs=(
            P("grp", "seq", None),
            P("grp", "seq", None),
            P("grp", "seq", None),
            P("grp", "seq", None),
            P("grp", "seq", None),
            P(),
            P(),
            P("grp", "seq", None),
        ),
        out_specs=(
            P("grp", "seq", None),
            P("grp", "seq", None),
            P("grp", "seq", None),
            P("grp", "seq", None),
            P(None, "seq"),
            P(None, "seq"),
        ),
        check_vma=False,
    )
```

profile of v0, /device:TPU:1, one launch (start us, length us, event | category | flops | bytes accessed | tf_op | source)
XLA Modules:
  0.0 414.7 jit_solution(14000686213218465211)
XLA Ops:
  9.7 8.5 %all-to-all-start = ((bf16[128,8,5,128]{0,3,2,1:T(8,128)(2,1)}), bf16[128,8,5,128]{0,3,2,1:T(8,128)(2,1)S(1)}, u32[]{:S(2)}, u32[]{:S(2)}) async-start(bf16[128,8,5,128]{0,3,2,1:T(8,128)(2,1)} %bitcast), calls=%async_computation | async-start | bytes 2621440 | tf_op jit(solution)/shard_map/all_to_all | solution.py:90
  21.4 7.9 %copy.145 = bf16[512,5120]{0,1:T(8,128)(2,1)} copy(bf16[512,5120]{1,0:T(8,128)(2,1)} %param.15) | data formatting | bytes 10485760 | tf_op jit(solution)/shard_map/reshape | solution.py:126
  29.3 10.0 %fusion.36 = (f32[40,128]{1,0:T(8,128)S(1)}, f32[40,128,512]{2,1,0:T(8,128)}) fusion(bf16[128,40,128]{0,2,1:T(8,128)(2,1)S(1)} %bitcast.198, bf16[512,40,128]{0,2,1:T(8,128)(2,1)} %bitcast.196), kind=kOutput, calls=%fused_computation.42 | convolution fusion | flops 678953472 | bytes 17059840 | tf_op jit(solution)/shard_map/while/body/eval_jaxpr/sub | solution.py:30
  39.3 6.6 %all-to-all-start.1 = ((bf16[128,8,5,128]{0,3,2,1:T(8,128)(2,1)}), bf16[128,8,5,128]{0,3,2,1:T(8,128)(2,1)}, u32[]{:S(2)}, u32[]{:S(2)}) async-start(bf16[128,8,5,128]{0,3,2,1:T(8,128)(2,1)} %bitcast.211), calls=%async_computation.1 | async-start | bytes 2621440 | tf_op jit(solution)/shard_map/all_to_all | solution.py:91
  46.0 7.3 %fusion.26 = bf16[40,128,512]{2,1,0:T(8,128)(2,1)} fusion(f32[40,128,512]{2,1,0:T(8,128)} %get-tuple-element.175, f32[40,128]{1,0:T(8,128)S(1)} %get-tuple-element.174), kind=kLoop, calls=%fused_computation.31 | loop fusion | flops 5242880 | bytes 15749120 | tf_op jit(solution)/shard_map/while/body/eval_jaxpr/convert_element_type | solution.py:31
  59.9 8.0 %copy.146 = bf16[512,5120]{0,1:T(8,128)(2,1)} copy(bf16[512,5120]{1,0:T(8,128)(2,1)} %param.16) | data formatting | bytes 10485760 | tf_op jit(solution)/shard_map/reshape | solution.py:127
  73.4 6.7 %all-to-all-start.2 = ((bf16[128,8,5,128]{0,3,2,1:T(8,128)(2,1)}), bf16[128,8,5,128]{0,3,2,1:T(8,128)(2,1)}, u32[]{:S(2)}, u32[]{:S(2)}) async-start(bf16[128,8,5,128]{0,3,2,1:T(8,128)(2,1)} %bitcast.212), calls=%async_computation.2 | async-start | bytes 2621440 | tf_op jit(solution)/shard_map/all_to_all | solution.py:93
  80.1 8.3 %multiply_convert_fusion.1 = bf16[40,128,512]{2,1,0:T(8,128)(2,1)} fusion(f32[40,128]{1,0:T(8,128)S(1)} %bitcast.223, f32[40,128,512]{2,1,0:T(8,128)} %get-tuple-element.175, f32[40,128]{1,0:T(8,128)S(1)} %get-tuple-element.174, bf16[128,40,128]{0,2,1:T(8,128)(2,1)S(1)} %bitcast.203, bf16[512,40,128]{0,2,1:T(8,128)(2,1)} %bitcast.208), kind=kOutput, calls=%fused_computation.25 | convolution fusion | flops 684195840 | bytes 22323200 | tf_op jit(solution)/shard_map/while/body/eval_jaxpr/nhe,mhe->hnm/dot_general | solution.py:34
  88.4 9.4 %all-to-all-done.2 = bf16[128,8,5,128]{0,3,2,1:T(8,128)(2,1)} async-done(((bf16[128,8,5,128]{0,3,2,1:T(8,128)(2,1)}), bf16[128,8,5,128]{0,3,2,1:T(8,128)(2,1)}, u32[]{:S(2)}, u32[]{:S(2)}) %all-to-all-start.2) | async-done | bytes 1310752 | tf_op jit(solution)/shard_map/all_to_all | solution.py:93
  102.6 7.8 %fusion.37 = f32[40,512,128]{1,2,0:T(8,128)} fusion(bf16[128,40,128]{0,2,1:T(8,128)(2,1)S(1)} %bitcast.199, bf16[40,128,512]{2,1,0:T(8,128)(2,1)} %multiply_convert_fusion.1), kind=kOutput, calls=%fused_computation.43 | convolution fusion | flops 671088640 | bytes 17039360 | tf_op jit(solution)/shard_map/while/body/eval_jaxpr/hgnm,gnhe->gmhe/dot_general | solution.py:47
  110.4 11.5 %copy.127 = f32[512,5120]{1,0:T(8,128)} copy(f32[512,5120]{0,1:T(8,128)} %bitcast.193) | data formatting | bytes 20971520 | tf_op jit(solution)/shard_map/reshape | solution.py:131
  121.9 8.0 %fusion.38 = f32[40,512,128]{1,2,0:T(8,128)} fusion(bf16[128,40,128]{0,2,1:T(8,128)(2,1)S(1)} %bitcast.204, bf16[40,128,512]{2,1,0:T(8,128)(2,1)} %fusion.26), kind=kOutput, calls=%fused_computation.44 | convolution fusion | flops 671088640 | bytes 17039360 | tf_op jit(solution)/shard_map/while/body/eval_jaxpr/hgnm,gnhe->gmhe/dot_general | solution.py:50
  129.8 11.5 %copy.128 = f32[512,5120]{1,0:T(8,128)} copy(f32[512,5120]{0,1:T(8,128)} %bitcast.192) | data formatting | bytes 20971520 | tf_op jit(solution)/shard_map/reshape | solution.py:132
  152.1 76.3 %while.3 = (s32[]{:T(128)}, f32[1024,5,128]{0,2,1:T(8,128)}, f32[1024,5,128]{0,2,1:T(8,128)}, bf16[2,512,5,128]{3,1,0,2:T(8,128)(2,1)}, bf16[2,512,5,128]{3,1,0,...) while((s32[]{:T(128)}, f32[1024,5,128]{0,2,1:T(8,128)}, ...), condition=%wide.region_4.0_spmd.clone, body=%wide.region_0.4_spmd.clone.sunk | while | flops 4056676864 | bytes 158648704 | solution.py:62
  153.5 8.6 %fusion.92 = (f32[5,512]{1,0:T(8,128)S(1)}, f32[5,512,1024]{2,1,0:T(8,128)}) fusion(bf16[1024,5,128]{2,0,1:T(8,128)(2,1)} %get-tuple-element.260, bf16[1,512,5,128]{3,1,0,2:T(8,128)(2,1)S(1)} %get-tuple-element.231), kind=kOutput, calls=%fused_computation.41.clone.1 | convolution fusion | flops 678953984 | bytes 12462080 | tf_op jit(solution)/shard_map/while/body/eval_jaxpr/sub | solution.py:30
  170.3 7.0 %multiply_convert_fusion.3 = bf16[5,512,1024]{2,1,0:T(8,128)(2,1)} fusion(f32[5,512]{1,0:T(8,128)S(1)} %bitcast.224, f32[5,512,1024]{2,1,0:T(8,128)} %get-tuple-element.232, f32[5,512]{1,0:T(8,128)S(1)} %get-tuple-element.233, bf16[1024,5,128]{0,2,1:T(8,128)(2,1)S(1)} %copy-done.7, bf16[1,512,5,128]{3,1,0,2:T(8,128)(2,1)S(1)} %get-tuple-element.234), kind=kOutput, calls=%fused_computation.1.clone.1 | convolution fusion | flops 684195840 | bytes 17715200 | tf_op jit(solution)/shard_map/while/body/eval_jaxpr/nhe,mhe->hnm/dot_general | solution.py:34
  190.7 8.5 %fusion.92 = (f32[5,512]{1,0:T(8,128)S(1)}, f32[5,512,1024]{2,1,0:T(8,128)}) fusion(bf16[1024,5,128]{2,0,1:T(8,128)(2,1)} %get-tuple-element.260, bf16[1,512,5,128]{3,1,0,2:T(8,128)(2,1)S(1)} %get-tuple-element.231), kind=kOutput, calls=%fused_computation.41.clone.1 | convolution fusion | flops 678953984 | bytes 12462080 | tf_op jit(solution)/shard_map/while/body/eval_jaxpr/sub | solution.py:30
  207.4 7.2 %multiply_convert_fusion.3 = bf16[5,512,1024]{2,1,0:T(8,128)(2,1)} fusion(f32[5,512]{1,0:T(8,128)S(1)} %bitcast.224, f32[5,512,1024]{2,1,0:T(8,128)} %get-tuple-element.232, f32[5,512]{1,0:T(8,128)S(1)} %get-tuple-element.233, bf16[1024,5,128]{0,2,1:T(8,128)(2,1)S(1)} %copy-done.7, bf16[1,512,5,128]{3,1,0,2:T(8,128)(2,1)S(1)} %get-tuple-element.234), kind=kOutput, calls=%fused_computation.1.clone.1 | convolution fusion | flops 684195840 | bytes 17715200 | tf_op jit(solution)/shard_map/while/body/eval_jaxpr/nhe,mhe->hnm/dot_general | solution.py:34
  214.6 6.2 %bitcast_add_fusion.4 = f32[1024,5,128]{0,2,1:T(8,128)} fusion(f32[1024,5,128]{0,2,1:T(8,128)} %get-tuple-element.246, bf16[4,128,5,128]{3,1,0,2:T(8,128)(2,1)S(1)} %bitcast.195, bf16[5,4,128,1024]{3,2,1,0:T(8,128)(2,1)} %bitcast.189, pred[]{:T(512)S(6)} %compare.3), kind=kOutput, calls=%fused_computation.9.clone.1 | convolution fusion | flops 672399360 | bytes 11141121 | tf_op jit(solution)/shard_map/while/body/eval_jaxpr/hgnm,gnhe->gmhe/dot_general | solution.py:47
  232.0 6.9 %all-to-all-start.4 = ((bf16[1024,1,5,128]{3,2,1,0:T(8,128)(2,1)}), bf16[1024,1,5,128]{3,2,1,0:T(8,128)(2,1)}, u32[]{:S(2)}, u32[]{:S(2)}) async-start(bf16[1024,1,5,128]{3,2,1,0:T(8,128)(2,1)} %copy.110), calls=%async_computation.4 | async-start | bytes 4194304 | tf_op jit(solution)/shard_map/all_to_all | solution.py:106
  242.0 23.9 %all-to-all-done.4 = bf16[1024,1,5,128]{3,2,1,0:T(8,128)(2,1)} async-done(((bf16[1024,1,5,128]{3,2,1,0:T(8,128)(2,1)}), bf16[1024,1,5,128]{3,2,1,0:T(8,128)(2,1)}, u32[]{:S(2)}, u32[]{:S(2)}) %all-to-all-start.4) | async-done | bytes 1310752 | tf_op jit(solution)/shard_map/all_to_all | solution.py:106
  274.5 24.0 %all-to-all-done.5 = bf16[1024,1,5,128]{3,2,1,0:T(8,128)(2,1)} async-done(((bf16[1024,1,5,128]{3,2,1,0:T(8,128)(2,1)}), bf16[1024,1,5,128]{3,2,1,0:T(8,128)(2,1)}, u32[]{:S(2)}, u32[]{:S(2)}) %all-to-all-start.5) | async-done | bytes 1310752 | tf_op jit(solution)/shard_map/all_to_all | solution.py:109
  322.5 14.6 %all-to-all-done.6 = bf16[1024,1,5,128]{3,2,1,0:T(8,128)(2,1)S(1)} async-done(((bf16[1024,1,5,128]{3,2,1,0:T(8,128)(2,1)}), bf16[1024,1,5,128]{3,2,1,0:T(8,128)(2,1)S(1)}, u32[]{:S(2)}, u32[]{:S(2)}) %all-to-all-start.6) | async-done | bytes 1310752 | tf_op jit(solution)/shard_map/all_to_all | solution.py:116
  339.5 65.0 %all-reduce.3.cloned.1.call-done = (f32[512,5120]{1,0:T(8,128)}, f32[512,5120]{1,0:T(8,128)}) async-done(((f32[512,5120]{1,0:T(8,128)}, f32[512,5120]{1,0:T(8,128)}), (f32[512,5120]{1,0:T(8,128)}, f32[512,5120]{1,0:T(8,128)})) %all-reduce.3.cloned.1.call-update) | async-done | bytes 20971536 | tf_op jit(solution)/shard_map/psum | solution.py:133
  (99 shorter events, 117.1 us)
Async XLA Ops:
  7.2 11.0 %copy-start.5 = (bf16[1,128,5120]{2,1,0:T(8,128)(2,1)S(1)}, bf16[1,128,5120]{2,1,0:T(8,128)(2,1)}, u32[]{:S(2)}) copy-start(bf16[1,128,5120]{2,1,0:T(8,128)(2,1)} %param.11) | copy-start | bytes 3932164
  9.7 29.6 %all-to-all-start = ((bf16[128,8,5,128]{0,3,2,1:T(8,128)(2,1)}), bf16[128,8,5,128]{0,3,2,1:T(8,128)(2,1)S(1)}, u32[]{:S(2)}, u32[]{:S(2)}) async-start(bf16[128,8,5,128]{0,3,2,1:T(8,128)(2,1)} %bitcast), calls=%async_computation | async-start | bytes 2621440 | tf_op jit(solution)/shard_map/all_to_all | solution.py:90
  39.3 13.9 %copy-start.3 = (bf16[128,8,5,128]{0,3,2,1:T(8,128)(2,1)}, bf16[128,8,5,128]{0,3,2,1:T(8,128)(2,1)S(1)}, u32[]{:S(2)}) copy-start(bf16[128,8,5,128]{0,3,2,1:T(8,128)(2,1)S(1)} %all-to-all-done) | copy-start | bytes 3932164
  39.3 34.1 %all-to-all-start.1 = ((bf16[128,8,5,128]{0,3,2,1:T(8,128)(2,1)}), bf16[128,8,5,128]{0,3,2,1:T(8,128)(2,1)}, u32[]{:S(2)}, u32[]{:S(2)}) async-start(bf16[128,8,5,128]{0,3,2,1:T(8,128)(2,1)} %bitcast.211), calls=%async_computation.1 | async-start | bytes 2621440 | tf_op jit(solution)/shard_map/all_to_all | solution.py:91
  73.4 24.4 %all-to-all-start.2 = ((bf16[128,8,5,128]{0,3,2,1:T(8,128)(2,1)}), bf16[128,8,5,128]{0,3,2,1:T(8,128)(2,1)}, u32[]{:S(2)}, u32[]{:S(2)}) async-start(bf16[128,8,5,128]{0,3,2,1:T(8,128)(2,1)} %bitcast.212), calls=%async_computation.2 | async-start | bytes 2621440 | tf_op jit(solution)/shard_map/all_to_all | solution.py:93
  97.9 51.0 %all-to-all-start.3 = ((bf16[128,8,5,128]{0,3,2,1:T(8,128)(2,1)}), bf16[128,8,5,128]{0,3,2,1:T(8,128)(2,1)}, u32[]{:S(2)}, u32[]{:S(2)}) async-start(bf16[128,8,5,128]{0,3,2,1:T(8,128)(2,1)} %bitcast.210), calls=%async_computation.3 | async-start | bytes 2621440 | tf_op jit(solution)/shard_map/all_to_all | solution.py:92
  102.4 302.1 %all-reduce.3.cloned.1.call-start = ((), (), s32[]{:S(2)}) async-start(), calls=%async_computation.7 | async-start | bytes 41943040 | tf_op jit(solution)/shard_map/psum | solution.py:133
  162.1 5.8 %copy-start.7 = (bf16[1024,5,128]{0,2,1:T(8,128)(2,1)S(1)}, bf16[1024,5,128]{0,2,1:T(8,128)(2,1)}, u32[]{:S(2)}) copy-start(bf16[1024,5,128]{0,2,1:T(8,128)(2,1)} %get-tuple-element.262) | copy-start | bytes 3932164 | tf_op jit(solution)/shard_map/while
  177.3 5.3 %slice-start = ((s8[5242880]{0:T(1024)(128)(4,1)}), s8[1048576]{0:T(1024)(128)(4,1)S(1)}, s32[]{:S(2)}) async-start(s8[5242880]{0:T(1024)(128)(4,1)} %bitcast.186), calls=%async_computation.8 | async-start | bytes 2097152 | tf_op jit(solution)/shard_map/while
  177.3 5.3 %slice-start.1 = ((s8[5242880]{0:T(1024)(128)(4,1)}), s8[4194304]{0:T(1024)(128)(4,1)S(1)}, s32[]{:S(2)}) async-start(s8[5242880]{0:T(1024)(128)(4,1)} %bitcast.186), calls=%async_computation.9 | async-start | bytes 8388608 | tf_op jit(solution)/shard_map/while
  177.3 7.9 %slice-start.2 = ((s8[5242880]{0:T(1024)(128)(4,1)}), s8[4194304]{0:T(1024)(128)(4,1)S(1)}, s32[]{:S(2)}) async-start(s8[5242880]{0:T(1024)(128)(4,1)} %bitcast.190), calls=%async_computation.10 | async-start | bytes 8388608 | tf_op jit(solution)/shard_map/while
  182.7 3.8 copy-start.8
  199.2 5.8 %copy-start.7 = (bf16[1024,5,128]{0,2,1:T(8,128)(2,1)S(1)}, bf16[1024,5,128]{0,2,1:T(8,128)(2,1)}, u32[]{:S(2)}) copy-start(bf16[1024,5,128]{0,2,1:T(8,128)(2,1)} %get-tuple-element.262) | copy-start | bytes 3932164 | tf_op jit(solution)/shard_map/while
  214.6 6.2 %slice-start = ((s8[5242880]{0:T(1024)(128)(4,1)}), s8[1048576]{0:T(1024)(128)(4,1)S(1)}, s32[]{:S(2)}) async-start(s8[5242880]{0:T(1024)(128)(4,1)} %bitcast.186), calls=%async_computation.8 | async-start | bytes 2097152 | tf_op jit(solution)/shard_map/while
  214.6 6.2 %slice-start.1 = ((s8[5242880]{0:T(1024)(128)(4,1)}), s8[4194304]{0:T(1024)(128)(4,1)S(1)}, s32[]{:S(2)}) async-start(s8[5242880]{0:T(1024)(128)(4,1)} %bitcast.186), calls=%async_computation.9 | async-start | bytes 8388608 | tf_op jit(solution)/shard_map/while
  214.6 11.0 %slice-start.2 = ((s8[5242880]{0:T(1024)(128)(4,1)}), s8[4194304]{0:T(1024)(128)(4,1)S(1)}, s32[]{:S(2)}) async-start(s8[5242880]{0:T(1024)(128)(4,1)} %bitcast.190), calls=%async_computation.10 | async-start | bytes 8388608 | tf_op jit(solution)/shard_map/while
  220.7 4.8 %slice-start.3 = ((s8[5242880]{0:T(1024)(128)(4,1)}), s8[1048576]{0:T(1024)(128)(4,1)S(1)}, s32[]{:S(2)}) async-start(s8[5242880]{0:T(1024)(128)(4,1)} %bitcast.190), calls=%async_computation.11 | async-start | bytes 2097152 | tf_op jit(solution)/shard_map/while
  220.8 4.8 %copy-start.6 = (bf16[1024,5,128]{2,0,1:T(8,128)(2,1)S(1)}, bf16[1024,5,128]{2,0,1:T(8,128)(2,1)}, u32[]{:S(2)}) copy-start(bf16[1024,5,128]{2,0,1:T(8,128)(2,1)} %get-tuple-element.260) | copy-start | bytes 3932164 | tf_op jit(solution)/shard_map/while
  220.8 4.8 %copy-start.8 = (bf16[2,512,5,128]{3,1,0,2:T(8,128)(2,1)S(1)}, bf16[2,512,5,128]{3,1,0,2:T(8,128)(2,1)}, u32[]{:S(2)}) copy-start(bf16[2,512,5,128]{3,1,0,2:T(8,128)(2,1)} %get-tuple-element.248) | copy-start | bytes 3932164 | tf_op jit(solution)/shard_map/while
  232.0 6.9 %copy-start.1 = (f32[1024,5,128]{0,2,1:T(8,128)S(1)}, f32[1024,5,128]{0,2,1:T(8,128)}, u32[]{:S(2)}) copy-start(f32[1024,5,128]{0,2,1:T(8,128)} %get-tuple-element.75) | copy-start | bytes 7864324
  232.0 33.9 %all-to-all-start.4 = ((bf16[1024,1,5,128]{3,2,1,0:T(8,128)(2,1)}), bf16[1024,1,5,128]{3,2,1,0:T(8,128)(2,1)}, u32[]{:S(2)}, u32[]{:S(2)}) async-start(bf16[1024,1,5,128]{3,2,1,0:T(8,128)(2,1)} %copy.110), calls=%async_computation.4 | async-start | bytes 4194304 | tf_op jit(solution)/shard_map/all_to_all | solution.py:106
  242.0 29.4 %copy-start.2 = (f32[1024,5,128]{0,2,1:T(8,128)S(1)}, f32[1024,5,128]{0,2,1:T(8,128)}, u32[]{:S(2)}) copy-start(f32[1024,5,128]{0,2,1:T(8,128)} %get-tuple-element.76) | copy-start | bytes 7864324
  265.9 32.7 %all-to-all-start.5 = ((bf16[1024,1,5,128]{3,2,1,0:T(8,128)(2,1)}), bf16[1024,1,5,128]{3,2,1,0:T(8,128)(2,1)}, u32[]{:S(2)}, u32[]{:S(2)}) async-start(bf16[1024,1,5,128]{3,2,1,0:T(8,128)(2,1)} %bitcast.206), calls=%async_computation.5 | async-start | bytes 4194304 | tf_op jit(solution)/shard_map/all_to_all | solution.py:109
  298.5 38.5 %all-to-all-start.6 = ((bf16[1024,1,5,128]{3,2,1,0:T(8,128)(2,1)}), bf16[1024,1,5,128]{3,2,1,0:T(8,128)(2,1)S(1)}, u32[]{:S(2)}, u32[]{:S(2)}) async-start(bf16[1024,1,5,128]{3,2,1,0:T(8,128)(2,1)} %bitcast.205), calls=%async_computation.6 | async-start | bytes 4194304 | tf_op jit(solution)/shard_map/all_to_all | solution.py:116
  (7 other events, 13.3 us)
Sparse Core Ops, SparseCore 0:
  141.5 262.9 all-reduce.2
where the time goes:
time: 416 us; the launch traced here: 415 us
  waiting for transfers between devices  137 us (33%)
  matrix products  102 us (25%)
  local copies, waits for them, and re-layouts  97.9 us (24%)
  starting transfers between devices  44.4 us (11%)
  other arithmetic  18.9 us (5%)
  between operations  14.2 us (3%)
    psum x1, waiting for transfers between devices, shards(): lax.psum((key_partial, value_partial), ('seq', 'grp'))  65 us
    sub x3, matrix products, advance(): weights = jax.nn.softmax(scores, axis=-1)  27.1 us
    all_to_all x1, waiting for transfers between devices, shards(): lax.all_to_all(key_part.astype(jnp.bfloat16).reshape(shape_back), 'seq',...  24 us
    all_to_all x1, waiting for transfers between devices, shards(): lax.all_to_all(query_part.reshape(shape_back), 'seq', split_axis=0, conca...  23.9 us
    dot_general x3, matrix products, advance(): jnp.einsum('nhe,mhe->hnm', upstream_block, value_in, preferred_element_ty...  22.5 us
    unnamed x20, local copies, waits for them, and re-layouts  21 us
    dot_general x3, matrix products, advance(): jnp.einsum('hgnm,gnhe->gmhe', score_split, query_split, preferred_element...  19.3 us
    convert_element_type x3, other arithmetic, advance(): rounded = weights.astype(jnp.bfloat16)  18.9 us
  transfers between devices with their start and end apart: 8, of which 5 were waited for; matrix products, arithmetic and copies ran while one was open for 50% of the time, Pallas kernels for 0%

commit v1 on v0

--- a/solution.py
+++ b/solution.py
@@ -130,7 +130,7 @@
     )
     key_partial = context_keys_part.reshape(text_rows, full_width)
     value_partial = context_values_part.reshape(text_rows, full_width)
-    key_whole, value_whole = lax.psum((key_partial, value_partial), ("seq", "grp"))
+    key_whole, value_whole = lax.psum(lax.psum((key_partial, value_partial), "seq"), "grp")
     key_total = lax.dynamic_slice_in_dim(key_whole, offset, columns, 1)
     value_total = lax.dynamic_slice_in_dim(value_whole, offset, columns, 1)
     shape_out = (1, token_count, full_width)

time: 416 us -> 1400 us (3.37)
  waiting for transfers between devices: 137 us -> 1150 us
    psum x1 -> x2, waiting for transfers between devices: 65 us -> 818 us  [the longest x1 818 us: shards(): lax.psum((key_partial, value_partial), 'seq')]
    all_to_all x1, waiting for transfers between devices: 0.01 us -> 123 us  [shards(): lax.all_to_all(to_groups(self_query[0]), 'seq', split_axis=1, concat_axis...]
    all_to_all x1, waiting for transfers between devices: 0.01 us -> 120 us  [shards(): lax.all_to_all(to_groups(self_key[0]), 'seq', split_axis=1, concat_axis=0...]
  transfers between devices with their start and end apart: 8 -> 9, of which waited for: 5 -> 8; matrix products, arithmetic and copies ran while one was open for 50% -> 8% of each run, Pallas kernels for 0% -> 0%
where the time goes in v1:
time: 1400 us; the launch traced here: 1390 us
  waiting for transfers between devices  1150 us (82%)
  local copies, waits for them, and re-layouts  94.5 us (7%)
  matrix products  90.5 us (6%)
  starting transfers between devices  33 us (2%)
  other arithmetic  16.4 us (1%)
  between operations  14.2 us (1%)
    psum x1, waiting for transfers between devices, shards(): lax.psum((key_partial, value_partial), 'seq')  818 us
    all_to_all x1, waiting for transfers between devices, shards(): lax.all_to_all(to_groups(self_query[0]), 'seq', split_axis=1, concat_axis...  123 us
    all_to_all x1, waiting for transfers between devices, shards(): lax.all_to_all(to_groups(self_key[0]), 'seq', split_axis=1, concat_axis=0...  120 us
  transfers between devices with their start and end apart: 9, of which 8 were waited for; matrix products, arithmetic and copies ran while one was open for 8% of the time, Pallas kernels for 0%

profile of v1, /device:TPU:1, one launch (start us, length us, event | category | flops | bytes accessed | tf_op | source)
XLA Modules:
  0.0 1394.9 jit_solution(16211632648935849451)
XLA Ops:
  10.8 7.9 copy.145
  18.7 7.9 copy.146
  26.6 9.8 fusion.36
  36.5 5.7 fusion.26
  42.1 5.5 fusion.38
  56.8 5.5 fusion.37
  62.3 11.5 copy.127
  73.8 11.5 copy.128
  85.5 818.2 %all-reduce.7.cloned.1.call-done = (f32[512,5120]{1,0:T(8,128)}, f32[512,5120]{1,0:T(8,128)}) async-done(((f32[512,5120]{1,0:T(8,128)}, f32[512,5120]{1,0:T(8,128)}), (f32[512,5120]{1,0:T(8,128)}, f32[512,5120]{1,0:T(8,128)})) %all-reduce.7.cloned.1.call-update) | async-done | bytes 20971536 | tf_op jit(solution)/shard_map/psum | solution.py:133
  912.7 123.0 %all-to-all-done = bf16[128,8,5,128]{0,3,2,1:T(8,128)(2,1)S(1)} async-done(((bf16[128,8,5,128]{0,3,2,1:T(8,128)(2,1)}), bf16[128,8,5,128]{0,3,2,1:T(8,128)(2,1)S(1)}, u32[]{:S(2)}, u32[]{:S(2)}) %all-to-all-start) | async-done | bytes 1310752 | tf_op jit(solution)/shard_map/all_to_all | solution.py:90
  1041.7 120.3 %all-to-all-done.1 = bf16[128,8,5,128]{0,3,2,1:T(8,128)(2,1)S(1)} async-done(((bf16[128,8,5,128]{0,3,2,1:T(8,128)(2,1)}), bf16[128,8,5,128]{0,3,2,1:T(8,128)(2,1)S(1)}, u32[]{:S(2)}, u32[]{:S(2)}) %all-to-all-start.1) | async-done | bytes 1310752 | tf_op jit(solution)/shard_map/all_to_all | solution.py:91
  1168.8 17.2 %all-to-all-done.2 = bf16[128,8,5,128]{0,3,2,1:T(8,128)(2,1)} async-done(((bf16[128,8,5,128]{0,3,2,1:T(8,128)(2,1)}), bf16[128,8,5,128]{0,3,2,1:T(8,128)(2,1)}, u32[]{:S(2)}, u32[]{:S(2)}) %all-to-all-start.2) | async-done | bytes 1310752 | tf_op jit(solution)/shard_map/all_to_all | solution.py:93
  1195.6 13.1 all-to-all-done.3
  1211.9 72.2 %while.3 = (s32[]{:T(128)}, f32[1024,5,128]{0,2,1:T(8,128)}, f32[1024,5,128]{0,2,1:T(8,128)}, bf16[2,512,5,128]{3,1,0,2:T(8,128)(2,1)}, bf16[2,512,5,128]{3,1,0,...) while((s32[]{:T(128)}, f32[1024,5,128]{0,2,1:T(8,128)}, ...), condition=%wide.region_4.0_spmd.clone, body=%wide.region_0.4_spmd.clone.sunk | while | flops 4056676864 | bytes 158648704 | solution.py:62
  1213.3 8.4 fusion.92
  1229.4 6.7 multiply_convert_fusion.3
  1248.0 8.4 fusion.92
  1264.2 6.7 multiply_convert_fusion.3
  1270.8 6.0 bitcast_add_fusion.4
  1295.5 22.8 %all-to-all-done.4 = bf16[1024,1,5,128]{3,2,1,0:T(8,128)(2,1)} async-done(((bf16[1024,1,5,128]{3,2,1,0:T(8,128)(2,1)}), bf16[1024,1,5,128]{3,2,1,0:T(8,128)(2,1)}, u32[]{:S(2)}, u32[]{:S(2)}) %all-to-all-start.4) | async-done | bytes 1310752 | tf_op jit(solution)/shard_map/all_to_all | solution.py:106
  1318.4 5.5 all-to-all-start.5
  1327.0 22.8 %all-to-all-done.5 = bf16[1024,1,5,128]{3,2,1,0:T(8,128)(2,1)} async-done(((bf16[1024,1,5,128]{3,2,1,0:T(8,128)(2,1)}), bf16[1024,1,5,128]{3,2,1,0:T(8,128)(2,1)}, u32[]{:S(2)}, u32[]{:S(2)}) %all-to-all-start.5) | async-done | bytes 1310752 | tf_op jit(solution)/shard_map/all_to_all | solution.py:109
  1355.4 5.6 convolution_convert_fusion.1
  1373.7 8.6 all-to-all-done.6
  (109 shorter events, 121.8 us)
Async XLA Ops:
  7.2 896.6 %all-reduce.7.cloned.1.call-start = ((), (), s32[]{:S(2)}) async-start(), calls=%async_computation.8 | async-start | bytes 41943040 | tf_op jit(solution)/shard_map/psum | solution.py:133
  36.5 15.5 %slice-start.4 = ((s8[10485760]{0:T(1024)(128)(4,1)}), s8[4194304]{0:T(1024)(128)(4,1)S(1)}, s32[]{:S(2)}) async-start(s8[10485760]{0:T(1024)(128)(4,1)} %bitcast.198), calls=%async_computation.13 | async-start | bytes 8388608
  42.1 9.8 slice-start.5
  42.1 9.8 slice-start.6
  56.8 5.5 copy-start.3
  85.3 1299.4 %all-reduce.5.cloned.1.call-start = ((), (), s32[]{:S(2)}) async-start(), calls=%async_computation.7 | async-start | bytes 41943040 | tf_op jit(solution)/shard_map/psum | solution.py:133
  905.0 6.2 copy-start.5
  906.5 129.3 %all-to-all-start = ((bf16[128,8,5,128]{0,3,2,1:T(8,128)(2,1)}), bf16[128,8,5,128]{0,3,2,1:T(8,128)(2,1)S(1)}, u32[]{:S(2)}, u32[]{:S(2)}) async-start(bf16[128,8,5,128]{0,3,2,1:T(8,128)(2,1)} %bitcast), calls=%async_computation | async-start | bytes 2621440 | tf_op jit(solution)/shard_map/all_to_all | solution.py:90
  1035.7 126.4 %all-to-all-start.1 = ((bf16[128,8,5,128]{0,3,2,1:T(8,128)(2,1)}), bf16[128,8,5,128]{0,3,2,1:T(8,128)(2,1)S(1)}, u32[]{:S(2)}, u32[]{:S(2)}) async-start(bf16[128,8,5,128]{0,3,2,1:T(8,128)(2,1)} %bitcast.214), calls=%async_computation.1 | async-start | bytes 2621440 | tf_op jit(solution)/shard_map/all_to_all | solution.py:91
  1162.1 23.9 %all-to-all-start.2 = ((bf16[128,8,5,128]{0,3,2,1:T(8,128)(2,1)}), bf16[128,8,5,128]{0,3,2,1:T(8,128)(2,1)}, u32[]{:S(2)}, u32[]{:S(2)}) async-start(bf16[128,8,5,128]{0,3,2,1:T(8,128)(2,1)} %bitcast.215), calls=%async_computation.2 | async-start | bytes 2621440 | tf_op jit(solution)/shard_map/all_to_all | solution.py:93
  1186.0 22.7 %all-to-all-start.3 = ((bf16[128,8,5,128]{0,3,2,1:T(8,128)(2,1)}), bf16[128,8,5,128]{0,3,2,1:T(8,128)(2,1)}, u32[]{:S(2)}, u32[]{:S(2)}) async-start(bf16[128,8,5,128]{0,3,2,1:T(8,128)(2,1)} %bitcast.213), calls=%async_computation.3 | async-start | bytes 2621440 | tf_op jit(solution)/shard_map/all_to_all | solution.py:92
  1221.7 5.4 copy-start.7
  1236.1 5.2 slice-start
  1236.1 5.2 slice-start.1
  1236.1 7.7 slice-start.2
  1256.5 5.4 copy-start.7
  1270.8 6.0 slice-start
  1270.8 6.0 slice-start.1
  1270.8 10.4 slice-start.2
  1287.7 4.8 copy-start.1
  1287.7 30.7 %all-to-all-start.4 = ((bf16[1024,1,5,128]{3,2,1,0:T(8,128)(2,1)}), bf16[1024,1,5,128]{3,2,1,0:T(8,128)(2,1)}, u32[]{:S(2)}, u32[]{:S(2)}) async-start(bf16[1024,1,5,128]{3,2,1,0:T(8,128)(2,1)} %copy.110), calls=%async_computation.4 | async-start | bytes 4194304 | tf_op jit(solution)/shard_map/all_to_all | solution.py:106
  1295.5 28.4 %copy-start.2 = (f32[1024,5,128]{0,2,1:T(8,128)S(1)}, f32[1024,5,128]{0,2,1:T(8,128)}, u32[]{:S(2)}) copy-start(f32[1024,5,128]{0,2,1:T(8,128)} %get-tuple-element.76) | copy-start | bytes 7864324
  1318.4 31.5 %all-to-all-start.5 = ((bf16[1024,1,5,128]{3,2,1,0:T(8,128)(2,1)}), bf16[1024,1,5,128]{3,2,1,0:T(8,128)(2,1)}, u32[]{:S(2)}, u32[]{:S(2)}) async-start(bf16[1024,1,5,128]{3,2,1,0:T(8,128)(2,1)} %bitcast.208), calls=%async_computation.5 | async-start | bytes 4194304 | tf_op jit(solution)/shard_map/all_to_all | solution.py:109
  1349.9 32.4 %all-to-all-start.6 = ((bf16[1024,1,5,128]{3,2,1,0:T(8,128)(2,1)}), bf16[1024,1,5,128]{3,2,1,0:T(8,128)(2,1)S(1)}, u32[]{:S(2)}, u32[]{:S(2)}) async-start(bf16[1024,1,5,128]{3,2,1,0:T(8,128)(2,1)} %bitcast.207), calls=%async_computation.6 | async-start | bytes 4194304 | tf_op jit(solution)/shard_map/all_to_all | solution.py:116
  (11 other events, 29.0 us)
Sparse Core Ops, SparseCore 0:
  85.4 818.2 all-reduce.6
  906.3 237.1 all-reduce.4
